TPU v7x, 256 devices: a whole 4x4x8 slice. The times are simulated.
256 devices in a mesh: dp: 32 (over y, x, core), mp: 8 (over z).
Axes of the slice: x: 4, y: 4, z: 8, core: 2. Of those that a mesh axis runs over, the one named last changes fastest.
Arguments:
- x_in: bfloat16 [16384, 2304], P(('dp', 'mp')), may hold values from -6 to 6
- out_grad: bfloat16 [16384, 2304], P(('dp', 'mp')), may hold values from -0.0625 to 0.0625
- context: bfloat16 [16384, 2048], P('dp', 'mp'), may hold values from -6 to 6
- query_grad: bfloat16 [16384, 2048], P('dp', 'mp'), may hold values from -0.0625 to 0.0625
- keyval_grad: bfloat16 [2, 16384, 1024], P(None, 'dp', 'mp'), may hold values from -0.0625 to 0.0625
- query_weight: bfloat16 [2304, 2048], P(None, 'mp'), may hold values from -2 to 2
- keyval_weight: bfloat16 [2, 2304, 1024], P(None, None, 'mp'), may hold values from -2 to 2
- wide_error: bfloat16 [32, 2, 2304, 2048], P('dp', None, None, 'mp'), may hold values from -1.1953125 to 1.1953125
- narrow_error: bfloat16 [32, 2, 2304, 1024], P('dp', None, None, 'mp'), may hold values from -1.1953125 to 1.1953125
- wide_start: float32 [2, 2048, 32], P(None, 'mp'), may hold values from -6 to 6
- narrow_start: float32 [2, 1024, 32], P(None, 'mp'), may hold values from -6 to 6
Outputs:
- input_grad: bfloat16 [16384, 2304], P(('dp', 'mp'))
- wide_p: float32 [2, 8, 2304, 32], P(None, 'mp', 'dp')
- narrow_p: float32 [2, 8, 2304, 32], P(None, 'mp', 'dp')
- wide_q: float32 [2, 2048, 32], P(None, 'mp')
- narrow_q: float32 [2, 1024, 32], P(None, 'mp')
- wide_error_new: bfloat16 [32, 2, 2304, 2048], P('dp', None, None, 'mp')
- narrow_error_new: bfloat16 [32, 2, 2304, 1024], P('dp', None, None, 'mp')
All inputs are finite; a program needn't handle non-finite values.
Results may differ from a plain program's by a relative error of at most 0.0016.
Values may be sent and summed in bfloat16 or wider, within the bound.
A program may use at most 128 MiB of HBM per device.

v0:
```python
import jax
import jax.numpy as jnp
from jax import lax
from jax.sharding import PartitionSpec as P

HIGH = lax.Precision.HIGHEST


def columns(factor):
    rank_size = factor.shape[2]
    col_order = jnp.arange(rank_size, dtype=jnp.int32)

    def advance(column_at, current):
        column_at = column_at.astype(jnp.int32)
        column = lax.dynamic_slice_in_dim(current, column_at, 1, 2)
        column = column / jnp.sqrt(jnp.sum(column * column, axis=1, keepdims=True))
        projected = jnp.sum(column * current, axis=1, keepdims=True)
        current = current - column * jnp.where(
            col_order > column_at, projected, jnp.zeros_like(projected)
        )
        return lax.dynamic_update_slice_in_dim(current, column, column_at, 2)

    return lax.fori_loop(jnp.int32(0), jnp.int32(rank_size), advance, factor)


def on_device(
    x_in,
    out_grad,
    context,
    query_grad,
    keyval_grad,
    query_weight,
    keyval_weight,
    wide_error,
    narrow_error,
    wide_start,
    narrow_start,
):
    cot_in = jnp.concatenate([query_grad, keyval_grad[0], keyval_grad[1]], axis=1)
    weight_in = jnp.concatenate([query_weight, keyval_weight[0], keyval_weight[1]], axis=1)
    width = x_in.shape[1]
    query_cols = query_grad.shape[1]
    keyval_cols = keyval_grad.shape[2]
    x_piece = lax.all_gather(x_in, "mp", axis=0, tiled=True)
    y_piece = lax.all_gather(out_grad, "mp", axis=0, tiled=True)
    cot_rows = cot_in
    grad_into = jnp.einsum("td,tc->dc", x_piece, cot_rows, preferred_element_type=jnp.float32)
    grad_outof = jnp.einsum("td,tc->dc", y_piece, context, preferred_element_type=jnp.float32)
    cot_rows = cot_in
    input_grad = lax.psum_scatter(
        jnp.einsum("tc,dc->td", cot_rows, weight_in, preferred_element_type=jnp.float32),
        "mp",
        scatter_dimension=0,
        tiled=True,
    ).astype(jnp.bfloat16)
    wide_sum = jnp.stack([grad_into[:, :query_cols], grad_outof]) + wide_error[0].astype(
        jnp.float32
    )
    narrow_sum = jnp.stack(
        [
            grad_into[:, query_cols : query_cols + keyval_cols],
            grad_into[:, query_cols + keyval_cols :],
        ]
    ) + narrow_error[0].astype(jnp.float32)
    factor_local = jnp.concatenate(
        [
            jnp.einsum("bdc,bcr->bdr", wide_sum, wide_start, precision=HIGH),
            jnp.einsum("bdc,bcr->bdr", narrow_sum, narrow_start, precision=HIGH),
        ],
        axis=0,
    )
    share_rows = width // lax.axis_size("dp")
    factor_sum = lax.psum(factor_local, "dp")
    factor_hat = columns(factor_sum)
    own_hat = lax.dynamic_slice_in_dim(factor_hat, lax.axis_index("dp") * share_rows, share_rows, 1)
    back_wide = jnp.einsum("bdc,bdr->bcr", wide_sum, factor_hat[:2], precision=HIGH)
    back_narrow = jnp.einsum("bdc,bdr->bcr", narrow_sum, factor_hat[2:], precision=HIGH)
    back_wide, back_narrow = lax.psum((back_wide, back_narrow), "dp")
    replicas = jnp.float32(lax.axis_size("dp"))
    wide_q = back_wide / replicas
    narrow_q = back_narrow / replicas
    wide_new = (
        wide_sum - jnp.einsum("bdr,bcr->bdc", factor_hat[:2], wide_q, precision=HIGH)
    ).astype(jnp.bfloat16)
    narrow_new = (
        narrow_sum - jnp.einsum("bdr,bcr->bdc", factor_hat[2:], narrow_q, precision=HIGH)
    ).astype(jnp.bfloat16)
    return (
        input_grad,
        own_hat[:2][:, None],
        own_hat[2:][:, None],
        wide_q,
        narrow_q,
        wide_new[None],
        narrow_new[None],
    )


def solution(mesh):
    return jax.shard_map(
        on_device,
        mesh=mesh,
        in_specs=(
            P(("dp", "mp"), None),
            P(("dp", "mp"), None),
            P("dp", "mp"),
            P("dp", "mp"),
            P(None, "dp", "mp"),
            P(None, "mp"),
            P(None, None, "mp"),
            P("dp", None, None, "mp"),
            P("dp", None, None, "mp"),
            P(None, "mp", None),
            P(None, "mp", None),
        ),
        out_specs=(
            P(("dp", "mp"), None),
            P(None, "mp", "dp", None),
            P(None, "mp", "dp", None),
            P(None, "mp", None),
            P(None, "mp", None),
            P("dp", None, None, "mp"),
            P("dp", None, None, "mp"),
        ),
        check_vma=False,
    )
```

profile of v0, /device:TPU:1, one launch (start us, length us, event | category | flops | bytes accessed | tf_op | source)
XLA Modules:
  0.0 442.2 jit_solution(14775877358113023925)
XLA Ops:
  8.7 2.4 copy.36
  11.1 2.9 copy.34
  14.1 38.2 %all-gather.3.cloned.1.call-done = bf16[512,2304]{1,0:T(8,128)(2,1)} async-done(((bf16[64,2304]{1,0:T(8,128)(2,1)}), bf16[512,2304]{1,0:T(8,128)(2,1)}) %all-gather.3.cloned.1.call-update) | async-done | bytes 2359312 | tf_op jit(solution)/shard_map/all_gather | solution.py:44
  52.3 3.1 convolution_bitcast_fusion
  55.6 1.4 copy-done.5
  57.0 1.5 fusion.18
  58.6 1.6 slice_bitcast_fusion
  60.1 34.3 %all-gather.5.cloned.1.call-done = bf16[512,2304]{1,0:T(8,128)(2,1)} async-done(((bf16[64,2304]{1,0:T(8,128)(2,1)}), bf16[512,2304]{1,0:T(8,128)(2,1)}) %all-gather.5.cloned.1.call-update) | async-done | bytes 2359312 | tf_op jit(solution)/shard_map/all_gather | solution.py:45
  94.4 2.6 convolution_bitcast_fusion.1
  97.1 3.2 fusion.17
  102.0 116.1 %all-reduce.3.cloned.1.call-done = f32[4,2304,32]{1,2,0:T(8,128)} async-done(((f32[4,2304,32]{1,2,0:T(8,128)}), f32[4,2304,32]{1,2,0:T(8,128)}) %all-reduce.3.cloned.1.call-update) | async-done | bytes 1179664 | tf_op jit(solution)/shard_map/psum | solution.py:73
  218.2 2.0 copy.38
  220.2 36.0 %while.11 = (s32[]{:T(128)}, f32[4,2304,32]{1,0,2:T(4,128)S(1)}, s32[]{:T(128)}) while((s32[]{:T(128)}, f32[4,2304,32]{1,0,2:T(4,128)S(1)}, s32[]{:T(128)}) %tuple.33), condition=%wide.region_5.6_spmd.clone, body=%wide.region_2.5_spmd.clone.sunk | while | flops 1216542 | bytes 6159037 | solution.py:23
  258.3 7.7 %fusion.15 = f32[2,256,32]{1,2,0:T(8,128)} fusion(f32[4,2304,32]{1,2,0:T(8,128)S(1)} %copy.39, f32[1,2304,256]{1,2,0:T(8,128)} %copy-done.4, f32[1,2304,256]{1,2,0:T(8,128)} %slice_bitcast_fusion, bf16[1,2,2304,256]{2,3,1,0:T(8,128)(2,1)S(1)} %copy-done.2), kind=kOutput, calls=%fused_computation.31 | convolution fusion | flops 456523776 | bytes 7733248 | tf_op jit(solution)/shard_map/bdc,bdr->bcr/dot_general | solution.py:76
  266.1 4.8 %fusion.7 = f32[512,2304]{1,0:T(8,128)} fusion(bf16[2304,128]{1,0:T(8,128)(2,1)S(1)} %get-tuple-element.58, bf16[2304,128]{1,0:T(8,128)(2,1)S(1)} %get-tuple-element.57, bf16[2304,256]{1,0:T(8,128)(2,1)} %param.18, bf16[512,128]{1,0:T(8,128)(2,1)S(1)} %get-tuple-element.60, bf16[512,128]{1,0:T(8,128)(2,1)S(1)} %get-tuple-element.59, ...), kind=kOutput, calls=%fused_computation.19 | convolution fusion | flops 1216610304 | bytes 7602176 | tf_op jit(solution)/shard_map/tc,dc->td/dot_general | solution.py:51
  272.2 4.3 fusion.13
  276.5 122.5 %psum.23 = f32[2,128,32]{1,2,0:T(8,128)S(1)} all-reduce(f32[2,128,32]{1,2,0:T(8,128)S(1)} %fusion.13), channel_id=1, replica_groups=mesh['dp'=32,'mp'=8] {'dp'}, use_global_device_ids=true, to_apply=%region_7.8 | all-reduce | flops 8192 | bytes 65536 | tf_op jit(solution)/shard_map/psum | solution.py:78
  399.0 4.8 %fusion.6 = bf16[1,2,2304,128]{2,3,1,0:T(8,128)(2,1)} fusion(f32[2,128,32]{1,2,0:T(8,128)S(1)} %broadcast_multiply_fusion.1, bf16[1,2,2304,128]{2,3,1,0:T(8,128)(2,1)S(1)} %copy-done.6, f32[1,2304,128]{1,2,0:T(8,128)} %copy-done.8, f32[1,2304,128]{1,2,0:T(8,128)} %copy-done.7, f32[4,2304,32]{1,0,2:T(4,128)S(1)} %get-tuple-element.24), kind=kOutput, calls=%fused_computation.17 | convolution fusion | flops 229441536 | bytes 5931008 | tf_op jit(solution)/shard_map/bdr,bcr->bdc/dot_general | solution.py:86
  403.8 2.4 copy.47
  406.2 1.6 dynamic-slice_bitcast_fusion
  408.6 7.3 %fusion.4 = bf16[1,2,2304,256]{2,3,1,0:T(8,128)(2,1)} fusion(f32[2,256,32]{1,2,0:T(8,128)S(1)} %broadcast_multiply_fusion, bf16[1,2,2304,256]{2,3,1,0:T(8,128)(2,1)} %copy-done.1, f32[1,2304,256]{1,2,0:T(8,128)} %copy-done.4, f32[1,2304,256]{1,2,0:T(8,128)} %slice_bitcast_fusion, f32[4,2304,32]{1,0,2:T(4,128)S(1)} %get-tuple-element.24), kind=kOutput, calls=%fused_computation.15 | convolution fusion | flops 458883072 | bytes 10682368 | tf_op jit(solution)/shard_map/bdr,bcr->bdc/dot_general | solution.py:83
  415.9 4.3 copy.46
  420.2 13.7 %reduce-scatter.2.cloned.1.call-done = f32[64,2304]{1,0:T(8,128)} async-done(((f32[512,2304]{1,0:T(8,128)}), f32[64,2304]{1,0:T(8,128)}) %reduce-scatter.2.cloned.1.call-update) | async-done | bytes 589840 | tf_op jit(solution)/shard_map/reduce_scatter | solution.py:50
  433.9 1.8 convert_element_type.21
  (341 shorter events, 42.5 us)
Async XLA Ops:
  7.2 87.2 %copy-start = (bf16[512,256]{1,0:T(8,128)(2,1)S(1)}, bf16[512,256]{1,0:T(8,128)(2,1)}, u32[]{:S(2)}) copy-start(bf16[512,256]{1,0:T(8,128)(2,1)} %param.15) | copy-start | bytes 786436
  7.2 45.1 %all-gather.3.cloned.1.call-start = ((), (), s32[]{:S(2)}) async-start(), calls=%async_computation.2 | async-start | bytes 2654208 | tf_op jit(solution)/shard_map/all_gather | solution.py:44
  7.9 86.5 %all-gather.5.cloned.1.call-start = ((), (), s32[]{:S(2)}) async-start(), calls=%async_computation.3 | async-start | bytes 2654208 | tf_op jit(solution)/shard_map/all_gather | solution.py:45
  8.7 209.5 %all-reduce.3.cloned.1.call-start = ((), (), s32[]{:S(2)}) async-start(), calls=%async_computation.4 | async-start | bytes 2359296 | tf_op jit(solution)/shard_map/psum | solution.py:73
  11.1 2.9 copy-start.12
  11.1 41.2 %copy-start.13 = (bf16[512,256]{1,0:T(8,128)(2,1)S(1)}, bf16[512,256]{1,0:T(8,128)(2,1)}, u32[]{:S(2)}) copy-start(bf16[512,256]{1,0:T(8,128)(2,1)} %param.16) | copy-start | bytes 786436
  14.0 83.0 %copy-start.1 = (bf16[1,2,2304,256]{2,3,1,0:T(8,128)(2,1)}, bf16[1,2,2304,256]{2,3,1,0:T(8,128)(2,1)S(1)}, u32[]{:S(2)}) copy-start(bf16[1,2,2304,256]{2,3,1,0:T(8,128)(2,1)S(1)} %copy.34) | copy-start | bytes 7077892
  55.4 1.7 copy-start.5
  55.4 1.6 copy-start.17
  55.6 3.0 copy-start.7
  55.6 3.0 copy-start.8
  60.1 36.9 %copy-start.16 = (f32[2,256,32]{1,2,0:T(8,128)S(1)}, f32[2,256,32]{1,2,0:T(8,128)}, u32[]{:S(2)}) copy-start(f32[2,256,32]{1,2,0:T(8,128)} %param.22) | copy-start | bytes 196612
  94.4 2.7 copy-start.3
  97.1 3.2 copy-start.4
  100.3 1.7 copy-start.10
  101.4 306.4 %all-reduce.5.cloned.1.call-start = ((), (), s32[]{:S(2)}) async-start(), calls=%async_computation.5 | async-start | bytes 131072 | tf_op jit(solution)/shard_map/psum | solution.py:78
  256.2 2.1 copy-start.2
  256.5 1.1 copy-start.9
  258.3 7.8 %copy-start.14 = (bf16[512,256]{1,0:T(8,128)(2,1)S(1)}, bf16[512,256]{1,0:T(8,128)(2,1)}, u32[]{:S(2)}) copy-start(bf16[512,256]{1,0:T(8,128)(2,1)} %param.16) | copy-start | bytes 786436
  266.1 167.8 %reduce-scatter.2.cloned.1.call-start = ((), (), s32[]{:S(2)}) async-start(), calls=%async_computation.1 | async-start | bytes 5308416 | tf_op jit(solution)/shard_map/reduce_scatter | solution.py:50
  270.9 1.3 copy-start.6
  399.0 4.8 %copy-start.15 = (f32[2,128,32]{1,2,0:T(8,128)}, f32[2,128,32]{1,2,0:T(8,128)S(1)}, u32[]{:S(2)}) copy-start(f32[2,128,32]{1,2,0:T(8,128)S(1)} %broadcast_multiply_fusion.1) | copy-start | bytes 98308
  408.6 7.3 %copy-start.11 = (f32[2,256,32]{1,2,0:T(8,128)}, f32[2,256,32]{1,2,0:T(8,128)S(1)}, u32[]{:S(2)}) copy-start(f32[2,256,32]{1,2,0:T(8,128)S(1)} %broadcast_multiply_fusion) | copy-start | bytes 196612
Sparse Core Ops, SparseCore 0:
  9.8 42.4 all-gather.2
  54.1 40.2 all-gather.4
  101.5 116.6 all-reduce.2
  266.2 105.9 all-reduce.4
  374.8 59.0 reduce-scatter.1
where the time goes:
time: 443 us; the launch traced here: 442 us
  waiting for transfers between devices  204 us (46%)
  blocking collectives  122 us (28%)
  matrix products  39.3 us (9%)
  other arithmetic  35.7 us (8%)
  local copies, waits for them, and re-layouts  25.3 us (6%)
  between operations  14 us (3%)
    psum x1, blocking collectives, on_device(): back_wide, back_narrow = lax.psum((back_wide, back_narrow), 'dp')  122 us
    psum x1, waiting for transfers between devices, on_device(): factor_sum = lax.psum(factor_local, 'dp')  116 us
    all_gather x1, waiting for transfers between devices, on_device(): x_piece = lax.all_gather(x_in, 'mp', axis=0, tiled=True)  38.2 us
    all_gather x1, waiting for transfers between devices, on_device(): y_piece = lax.all_gather(out_grad, 'mp', axis=0, tiled=True)  34.3 us
    unnamed x41, local copies, waits for them, and re-layouts  18.9 us
    reduce_scatter x1, waiting for transfers between devices, on_device(): lax.psum_scatter(jnp.einsum('tc,dc->td', cot_rows, weight_in, preferred_e...  13.7 us
    reduce_sum x32, other arithmetic, advance(): projected = jnp.sum(column * current, axis=1, keepdims=True)  10.4 us
    sub x32, other arithmetic, advance(): current - column * jnp.where(col_order > column_at, projected, jnp.zeros_...  9.28 us
  transfers between devices with their start and end apart: 5, of which 4 were waited for; matrix products, arithmetic and copies ran while one was open for 9% of the time, Pallas kernels for 0%

commit v1 on v0

v1 whole, which is shorter than its diff:
```python
import jax
import jax.numpy as jnp
from jax import lax
from jax.experimental import pallas as pl
from jax.experimental.pallas import tpu as pltpu
from jax.sharding import PartitionSpec as P

MESH = pl.DeviceIdType.MESH
F32 = jnp.float32
BF16 = jnp.bfloat16

D = 2304
HALF = D // 2
TOK = 512
SHARE = 64
PART = SHARE // 2
RANK = 32
N_DP = 32
N_MP = 8
CHIPS = N_DP // 2
ROWS_P = D // N_DP
COLS = ((0, 256), (256, 128), (384, 128), (512, 256))
INTO = 512
ALL = 768


def split(value):
    high = value.astype(BF16)
    return high, (value - high.astype(F32)).astype(BF16)


def dot(a, b, on_a=1, on_b=0):
    return lax.dot_general(a, b, (((on_a,), (on_b,)), ((), ())), preferred_element_type=F32)


def kernel(
    x_in, out_grad, context, query_grad, keyval_grad, query_weight, keyval_weight,
    wide_error, narrow_error, wide_start, narrow_start,
    input_grad, wide_p, narrow_p, wide_q, narrow_q, wide_new, narrow_new,
    xf, yf, gv, wv, ev, sw, sn, st, tx, ty, pg, rr, sh, sl,
    fl, ra, rb, ff, rowbuf, pb, pt, pc, ql, rq, qf, qbd, nv, ig, pst, qsw, qsn,
    load_sem, x_send, x_recv, y_send, y_recv, z_send, z_recv,
    a_send, a_recv, b_send, b_recv, c_send, c_recv, d_send, d_recv,
    e_send, e_recv, f_send, f_recv, out_sem, small_sem,
):
    dp = lax.axis_index("dp")
    mp = lax.axis_index("mp")
    core = dp % 2
    chip = dp // 2
    mate = dp + 1 - 2 * core
    ring = ((mp + 1) % N_MP, (mp + N_MP - 1) % N_MP)

    def along(way, steps):
        return (mp + steps) % N_MP if way == 0 else (mp + N_MP - steps) % N_MP

    loads = [
        (query_grad, gv.at[:, 0:256]),
        (keyval_grad.at[0], gv.at[:, 256:384]),
        (keyval_grad.at[1], gv.at[:, 384:512]),
        (query_weight, wv.at[:, 0:256]),
        (keyval_weight.at[0], wv.at[:, 256:384]),
        (keyval_weight.at[1], wv.at[:, 384:512]),
        (wide_start, sw),
        (narrow_start, sn),
        (wide_error.at[0, 0], ev.at[:, 0:256]),
        (narrow_error.at[0, 0], ev.at[:, 256:384]),
        (narrow_error.at[0, 1], ev.at[:, 384:512]),
        (wide_error.at[0, 1], ev.at[:, 512:768]),
        (context, gv.at[:, 512:768]),
        (x_in, xf.at[pl.ds(pl.multiple_of(mp * SHARE, SHARE), SHARE), :]),
        (out_grad, yf.at[pl.ds(pl.multiple_of(mp * SHARE, SHARE), SHARE), :]),
    ]
    loads = [pltpu.make_async_copy(a, b, load_sem.at[i]) for i, (a, b) in enumerate(loads)]
    for copy in loads:
        copy.start()

    barrier = pltpu.get_barrier_semaphore()
    for way in (0, 1):
        pl.semaphore_signal(barrier, inc=1, device_id=(dp, ring[way]), device_id_type=MESH)

    @pl.loop(1, N_DP)
    def _(k):
        pl.semaphore_signal(barrier, inc=1, device_id=((dp + k) % N_DP, mp), device_id_type=MESH)

    pl.semaphore_wait(barrier, N_DP + 1)

    def hop(own, full, send, recv, way, step, role):
        part = way if role == 0 else 1 - way
        owner = along(1 - way, step - 1)
        rows = pl.ds(pl.multiple_of(owner * SHARE + part * PART, PART), PART)
        src = own.at[part * PART:(part + 1) * PART, :] if step == 1 else full.at[rows, :]
        return pltpu.make_async_remote_copy(
            src_ref=src, dst_ref=full.at[rows, :],
            send_sem=send.at[way, step - 1, role], recv_sem=recv.at[way, step - 1, role],
            device_id=(dp, ring[way]), device_id_type=MESH,
        )

    def x_hop(way, step, role):
        return hop(x_in, xf, x_send, x_recv, way, step, role)

    def y_hop(way, step, role):
        return hop(out_grad, yf, y_send, y_recv, way, step, role)

    def first(make):
        for role in (0, 1):
            for way in (0, 1):
                make(way, 1, role).start()

    def forward(make, step, role):
        for way in (0, 1):
            make(way, step - 1, role).wait_recv()
            make(way, step, role).start()

    def finish_ring(make):
        for way in (0, 1):
            make(way, 3, 1).wait_recv()
            make(way, 4, 0).wait_recv()

    def drain_ring(make):
        for way in (0, 1):
            for step in (1, 2, 3, 4):
                for role in (0, 1):
                    if (step, role) != (4, 1):
                        make(way, step, role).wait_send()

    def z_hop(way, step, role):
        part = way if role == 0 else 1 - way
        dest = along(way, 5 - step)
        rows = pl.ds(pl.multiple_of(dest * SHARE + part * PART, PART), PART)
        here = slice(part * PART, (part + 1) * PART)
        if step == (1 if role == 0 else 2):
            src = pg.at[rows, :]
        else:
            src = rr.at[way, step - 2, here, :]
        return pltpu.make_async_remote_copy(
            src_ref=src, dst_ref=rr.at[way, step - 1, here, :],
            send_sem=z_send.at[way, step - 1, role], recv_sem=z_recv.at[way, step - 1, role],
            device_id=(dp, ring[way]), device_id_type=MESH,
        ), rows, here

    def z_first():
        for way in (0, 1):
            z_hop(way, 1, 0)[0].start()
        for way in (0, 1):
            z_hop(way, 2, 1)[0].start()

    def z_step(step, role):
        for way in (0, 1):
            z_hop(way, step - 1, role)[0].wait_recv()
            copy, rows, here = z_hop(way, step, role)
            rr[way, step - 2, here, :] += pg[rows, :]
            copy.start()

    first(x_hop)
    for i in range(6):
        loads[i].wait()

    @pl.loop(0, 9)
    def _(j):
        cols = pl.ds(pl.multiple_of(j * 256, 256), 256)
        pg[:, cols] = dot(gv[:, 0:INTO], wv[cols, :], 1, 1)

    forward(x_hop, 2, 0)
    forward(x_hop, 2, 1)

    for i in (6, 7):
        loads[i].wait()
    for b, (at, width) in enumerate(COLS):
        start = sw[0 if b == 0 else 1] if width == 256 else sn[b - 1]
        high, low = split(jnp.transpose(start))
        st[0:RANK, at:at + width] = high
        st[RANK:2 * RANK, at:at + width] = low
    loads[12].wait()
    for b, (at, width) in enumerate(COLS):
        t = dot(st[:, at:at + width], gv[:, at:at + width], 1, 1)
        high, low = split(t[:RANK] + t[RANK:])
        if b < 3:
            tx[b * RANK:(b + 1) * RANK, :] = high
            tx[96 + b * RANK:96 + (b + 1) * RANK, :] = low
        else:
            ty[0:RANK, :] = high
            ty[RANK:2 * RANK, :] = low
    qbd[...] = jnp.zeros_like(qbd)
    ql[:, ALL:] = jnp.zeros((RANK, 1024 - ALL), F32)

    forward(x_hop, 3, 0)
    forward(x_hop, 3, 1)

    for i in (8, 9, 10, 11):
        loads[i].wait()

    @pl.loop(0, 6)
    def _(j):
        rows = pl.ds(pl.multiple_of(j * 384, 384), 384)
        lanes = pl.ds(pl.multiple_of((j % 3) * 384, 384), 384)
        for b, (at, width) in enumerate(COLS):
            e = dot(st[:, at:at + width], ev[rows, at:at + width], 1, 1)
            fl[j // 3, b * RANK:(b + 1) * RANK, lanes] = e[:RANK] + e[RANK:]

    forward(x_hop, 4, 0)
    first(y_hop)
    loads[13].wait()
    finish_ring(x_hop)

    @pl.loop(0, 6)
    def _(j):
        cols = pl.ds(pl.multiple_of(j * 384, 384), 384)
        lanes = pl.ds(pl.multiple_of((j % 3) * 384, 384), 384)
        f = dot(tx[...], xf[:, cols])
        fl[j // 3, 0:96, lanes] += f[:96] + f[96:]

    forward(y_hop, 2, 0)
    forward(y_hop, 2, 1)

    @pl.loop(0, 9)
    def _(j):
        rows = pl.ds(pl.multiple_of(j * 256, 256), 256)
        total = dot(xf[:, rows], gv[:, 0:INTO], 0, 0) + ev[rows, 0:INTO].astype(F32)
        high, low = split(total)
        sh[rows, 0:INTO] = high
        sl[rows, 0:INTO] = low

    forward(y_hop, 3, 0)
    forward(y_hop, 3, 1)
    forward(y_hop, 4, 0)
    z_first()
    loads[14].wait()
    finish_ring(y_hop)

    @pl.loop(0, 6)
    def _(j):
        cols = pl.ds(pl.multiple_of(j * 384, 384), 384)
        lanes = pl.ds(pl.multiple_of((j % 3) * 384, 384), 384)
        f = dot(ty[...], yf[:, cols])
        fl[j // 3, 96:128, lanes] += f[:RANK] + f[RANK:]

    a_copy = pltpu.make_async_remote_copy(
        src_ref=fl.at[1 - core], dst_ref=ra, send_sem=a_send, recv_sem=a_recv,
        device_id=(mate, mp), device_id_type=MESH,
    )
    a_copy.start()

    @pl.loop(0, 9)
    def _(j):
        rows = pl.ds(pl.multiple_of(j * 256, 256), 256)
        total = dot(yf[:, rows], gv[:, INTO:ALL], 0, 0) + ev[rows, INTO:ALL].astype(F32)
        high, low = split(total)
        sh[rows, INTO:ALL] = high
        sl[rows, INTO:ALL] = low

    a_copy.wait_recv()
    fl[core] += ra[...]

    def b_copy(k):
        other = (chip + k) % CHIPS
        return pltpu.make_async_remote_copy(
            src_ref=fl.at[core, pl.ds(pl.multiple_of(other * 8, 8), 8), :], dst_ref=rb.at[k - 1],
            send_sem=b_send.at[k - 1], recv_sem=b_recv.at[k - 1],
            device_id=(2 * other + core, mp), device_id_type=MESH,
        )

    own_rows = pl.ds(pl.multiple_of(chip * 8, 8), 8)

    def c_copy(k):
        other = (chip + k) % CHIPS
        own = ff.at[core, own_rows, :]
        return pltpu.make_async_remote_copy(
            src_ref=own, dst_ref=own,
            send_sem=c_send.at[k - 1], recv_sem=c_recv.at[k - 1],
            device_id=(2 * other + core, mp), device_id_type=MESH,
        )

    @pl.loop(1, CHIPS)
    def _(k):
        b_copy(k).start()

    z_step(2, 0)

    @pl.loop(1, CHIPS)
    def _(k):
        b_copy(k).wait_recv()

    ff[core, own_rows, :] = fl[core, own_rows, :] + jnp.sum(rb[...], axis=0)

    @pl.loop(1, CHIPS)
    def _(k):
        c_copy(k).start()

    z_step(3, 1)

    @pl.loop(1, CHIPS)
    def _(k):
        c_copy(k).wait_recv()

    d_copy = pltpu.make_async_remote_copy(
        src_ref=ff.at[core], dst_ref=ff.at[core], send_sem=d_send, recv_sem=d_recv,
        device_id=(mate, mp), device_id_type=MESH,
    )
    d_copy.start()
    z_step(3, 0)
    a_copy.wait_send()

    @pl.loop(1, CHIPS)
    def _(k):
        b_copy(k).wait_send()
        c_copy(k).wait_send()

    d_copy.wait()

    def gram_schmidt(block):
        @pl.loop(0, 8)
        def _(i):
            norms = []
            for b in range(4):
                row = [ff[h, pl.ds(b * RANK + block * 8 + i, 1), :] for h in (0, 1)]
                for h in (0, 1):
                    rowbuf[h, b * 8:b * 8 + 8, :] = jnp.broadcast_to(row[h], (8, HALF))
                norms.append(jnp.sum(row[0] * row[0] + row[1] * row[1], axis=1, keepdims=True))
            later = lax.broadcasted_iota(jnp.int32, (8, 1), 0) > i
            scales = {}
            for b in range(4):
                for t in range(block, 4):
                    at = slice(b * RANK + t * 8, b * RANK + t * 8 + 8)
                    r = slice(b * 8, b * 8 + 8)
                    dots = jnp.sum(
                        ff[0, at, :] * rowbuf[0, r, :] + ff[1, at, :] * rowbuf[1, r, :],
                        axis=1, keepdims=True,
                    )
                    scale = dots / norms[b]
                    scales[b, t] = jnp.where(later, scale, 0.0) if t == block else scale
            for b in range(4):
                for t in range(block, 4):
                    at = slice(b * RANK + t * 8, b * RANK + t * 8 + 8)
                    for h in (0, 1):
                        ff[h, at, :] -= scales[b, t] * rowbuf[h, b * 8:b * 8 + 8, :]

    gram_schmidt(0)
    gram_schmidt(1)
    z_step(4, 1)
    gram_schmidt(2)
    gram_schmidt(3)
    for b in range(4):
        at = slice(b * RANK, (b + 1) * RANK)
        squares = jnp.sum(ff[0, at, :] * ff[0, at, :] + ff[1, at, :] * ff[1, at, :], axis=1, keepdims=True)
        size = jnp.sqrt(squares)
        for h in (0, 1):
            unit = ff[h, at, :] / size
            ff[h, at, :] = unit
            high, low = split(unit)
            pb[2 * b * RANK:(2 * b + 1) * RANK, h * HALF:(h + 1) * HALF] = high
            pb[(2 * b + 1) * RANK:(2 * b + 2) * RANK, h * HALF:(h + 1) * HALF] = low

    for b, (at, width) in enumerate(COLS):
        both = dot(pb[2 * b * RANK:(2 * b + 2) * RANK, :], sh[:, at:at + width])
        rest = dot(pb[2 * b * RANK:(2 * b + 1) * RANK, :], sl[:, at:at + width])
        ql[:, at:at + width] = both[:RANK] + both[RANK:] + rest

    def tile_of(j):
        return (
            pl.ds(pl.multiple_of((j % 4) * 8, 8), 8),
            pl.ds(pl.multiple_of((j // 4) * 128, 128), 128),
        )

    own_tile = tile_of(dp)

    def e_copy(k):
        other = (dp + k) % N_DP
        tile = tile_of(other)
        return pltpu.make_async_remote_copy(
            src_ref=ql.at[tile[0], tile[1]], dst_ref=rq.at[k - 1],
            send_sem=e_send.at[k - 1], recv_sem=e_recv.at[k - 1],
            device_id=(other, mp), device_id_type=MESH,
        )

    def f_copy(k):
        own = qf.at[own_tile[0], own_tile[1]]
        return pltpu.make_async_remote_copy(
            src_ref=own, dst_ref=own,
            send_sem=f_send.at[k - 1], recv_sem=f_recv.at[k - 1],
            device_id=((dp + k) % N_DP, mp), device_id_type=MESH,
        )

    @pl.loop(1, N_DP)
    def _(k):
        e_copy(k).start()

    z_step(4, 0)

    @pl.loop(1, N_DP)
    def _(k):
        e_copy(k).wait_recv()

    qf[own_tile[0], own_tile[1]] = (
        ql[own_tile[0], own_tile[1]] + jnp.sum(rq[...], axis=0)
    ) * (1.0 / N_DP)

    @pl.loop(1, N_DP)
    def _(k):
        f_copy(k).start()

    for h in (0, 1):
        @pl.loop(0, 3)
        def _(j):
            lanes = pl.ds(pl.multiple_of(j * 384, 384), 384)
            rows = pl.ds(pl.multiple_of(h * HALF + j * 384, 384), 384)
            by_row = jnp.transpose(ff[h, :, lanes])
            pt[rows, :] = by_row
            high, low = split(by_row)
            pc[rows, 0:128] = high
            pc[rows, 128:256] = high
            pc[rows, 256:384] = low

    mine = pt[pl.ds(pl.multiple_of(dp * ROWS_P, 8), ROWS_P), :]
    for b in range(4):
        pst[b] = mine[:, b * RANK:(b + 1) * RANK]
    small = [
        pltpu.make_async_copy(pst.at[b], dst, small_sem.at[b])
        for b, dst in enumerate((wide_p.at[0, 0], narrow_p.at[0, 0], narrow_p.at[1, 0], wide_p.at[1, 0]))
    ]
    for copy in small:
        copy.start()

    @pl.loop(1, N_DP)
    def _(k):
        f_copy(k).wait_recv()

    for b, (at, width) in enumerate(COLS):
        q = qf[:, at:at + width]
        high, low = split(q)
        qbd[b * RANK:(b + 1) * RANK, at:at + width] = high
        qbd[128 + b * RANK:128 + (b + 1) * RANK, at:at + width] = low
        qbd[256 + b * RANK:256 + (b + 1) * RANK, at:at + width] = high

    def out_copies(j):
        rows = pl.ds(pl.multiple_of(j * 256, 256), 256)
        targets = (wide_new.at[0, 0], narrow_new.at[0, 0], narrow_new.at[0, 1], wide_new.at[0, 1])
        return [
            pltpu.make_async_copy(nv.at[rows, at:at + width], targets[b].at[rows, :], out_sem.at[j, b])
            for b, (at, width) in enumerate(COLS)
        ]

    @pl.loop(0, 9)
    def _(j):
        rows = pl.ds(pl.multiple_of(j * 256, 256), 256)
        low_rank = dot(pc[rows, :], qbd[...])
        nv[rows, :] = (sh[rows, :].astype(F32) + sl[rows, :].astype(F32) - low_rank).astype(BF16)
        for copy in out_copies(j):
            copy.start()

    for b, (at, width) in enumerate(COLS):
        by_row = jnp.transpose(qf[:, at:at + width])
        if width == 256:
            qsw[0 if b == 0 else 1] = by_row
        else:
            qsn[b - 1] = by_row
    tail = [
        pltpu.make_async_copy(qsw, wide_q, small_sem.at[4]),
        pltpu.make_async_copy(qsn, narrow_q, small_sem.at[5]),
    ]
    for copy in tail:
        copy.start()

    for way in (0, 1):
        for role in (0, 1):
            z_hop(way, 4, role)[0].wait_recv()
    own = pl.ds(pl.multiple_of(mp * SHARE, SHARE), SHARE)
    ig[...] = (pg[own, :] + rr[0, 3] + rr[1, 3]).astype(BF16)
    last = pltpu.make_async_copy(ig, input_grad, small_sem.at[6])
    last.start()

    drain_ring(x_hop)
    drain_ring(y_hop)
    for way in (0, 1):
        for step in (1, 2, 3, 4):
            for role in (0, 1):
                if (step, role) != (1, 1):
                    z_hop(way, step, role)[0].wait_send()

    @pl.loop(1, N_DP)
    def _(k):
        e_copy(k).wait_send()
        f_copy(k).wait_send()

    for copy in small + tail:
        copy.wait()

    @pl.loop(0, 9)
    def _(j):
        for copy in out_copies(j):
            copy.wait()

    last.wait()


def on_device(*args):
    sems = pltpu.SemaphoreType.DMA
    vmem = pltpu.VMEM
    return pl.pallas_call(
        kernel,
        out_shape=(
            jax.ShapeDtypeStruct((SHARE, D), BF16),
            jax.ShapeDtypeStruct((2, 1, ROWS_P, RANK), F32),
            jax.ShapeDtypeStruct((2, 1, ROWS_P, RANK), F32),
            jax.ShapeDtypeStruct((2, 256, RANK), F32),
            jax.ShapeDtypeStruct((2, 128, RANK), F32),
            jax.ShapeDtypeStruct((1, 2, D, 256), BF16),
            jax.ShapeDtypeStruct((1, 2, D, 128), BF16),
        ),
        in_specs=[pl.BlockSpec(memory_space=pl.ANY)] * 11,
        out_specs=tuple([pl.BlockSpec(memory_space=pl.ANY)] * 7),
        scratch_shapes=[
            vmem((TOK, D), BF16),
            vmem((TOK, D), BF16),
            vmem((TOK, ALL), BF16),
            vmem((D, INTO), BF16),
            vmem((D, ALL), BF16),
            vmem((2, 256, RANK), F32),
            vmem((2, 128, RANK), F32),
            vmem((2 * RANK, ALL), BF16),
            vmem((192, TOK), BF16),
            vmem((64, TOK), BF16),
            vmem((TOK, D), F32),
            vmem((2, 4, SHARE, D), F32),
            vmem((D, ALL), BF16),
            vmem((D, ALL), BF16),
            vmem((2, 128, HALF), F32),
            vmem((128, HALF), F32),
            vmem((CHIPS - 1, 8, HALF), F32),
            vmem((2, 128, HALF), F32),
            vmem((2, 32, HALF), F32),
            vmem((256, D), BF16),
            vmem((D, 128), F32),
            vmem((D, 384), BF16),
            vmem((RANK, 1024), F32),
            vmem((N_DP - 1, 8, 128), F32),
            vmem((RANK, 1024), F32),
            vmem((384, ALL), BF16),
            vmem((D, ALL), BF16),
            vmem((SHARE, D), BF16),
            vmem((4, ROWS_P, RANK), F32),
            vmem((2, 256, RANK), F32),
            vmem((2, 128, RANK), F32),
            sems((15,)),
            sems((2, 4, 2)), sems((2, 4, 2)),
            sems((2, 4, 2)), sems((2, 4, 2)),
            sems((2, 4, 2)), sems((2, 4, 2)),
            sems, sems,
            sems((CHIPS - 1,)), sems((CHIPS - 1,)),
            sems((CHIPS - 1,)), sems((CHIPS - 1,)),
            sems, sems,
            sems((N_DP - 1,)), sems((N_DP - 1,)),
            sems((N_DP - 1,)), sems((N_DP - 1,)),
            sems((9, 4)),
            sems((7,)),
        ],
        compiler_params=pltpu.CompilerParams(
            collective_id=0, has_side_effects=True, vmem_limit_bytes=58 * 1024 * 1024
        ),
    )(*args)


def solution(mesh):
    return jax.shard_map(
        on_device,
        mesh=mesh,
        in_specs=(
            P(("dp", "mp"), None),
            P(("dp", "mp"), None),
            P("dp", "mp"),
            P("dp", "mp"),
            P(None, "dp", "mp"),
            P(None, "mp"),
            P(None, None, "mp"),
            P("dp", None, None, "mp"),
            P("dp", None, None, "mp"),
            P(None, "mp", None),
            P(None, "mp", None),
        ),
        out_specs=(
            P(("dp", "mp"), None),
            P(None, "mp", "dp", None),
            P(None, "mp", "dp", None),
            P(None, "mp", None),
            P(None, "mp", None),
            P("dp", None, None, "mp"),
            P("dp", None, None, "mp"),
        ),
        check_vma=False,
    )
```

time: 443 us -> 124 us (0.28)
  waiting for transfers between devices: 204 us -> 0 us
  blocking collectives: 122 us -> 0 us
  Pallas kernels: 0 us -> 107 us
  matrix products: 39.3 us -> 0 us
  other arithmetic: 35.7 us -> 0 us
  between operations: 14 us -> 0.65 us
  local copies, waits for them, and re-layouts: 25.3 us -> 15.6 us
    psum x1 -> x0, blocking collectives: 122 us -> none  [on_device(): back_wide, back_narrow = lax.psum((back_wide, back_narrow), 'dp')]
    psum x2 -> x0, waiting for transfers between devices: 116 us -> none  [the longest x1 116 us: on_device(): factor_sum = lax.psum(factor_local, 'dp')]
    pallas_call x0 -> x1, Pallas kernels: none -> 107 us  [on_device(): pl.pallas_call(kernel, out_shape=(jax.ShapeDtypeStruct((SHARE, D), BF16),...]
    all_gather x2 -> x0, waiting for transfers between devices: 72.5 us -> none  [the longest x1 38.2 us: on_device(): x_piece = lax.all_gather(x_in, 'mp', axis=0, tiled=True)]
    dot_general x9 -> x0, matrix products: 39.3 us -> none  [the longest x1 7.73 us: on_device(): jnp.einsum('bdc,bdr->bcr', wide_sum, factor_hat[:2], precision=HIGH)]
    reduce_sum x64 -> x0, other arithmetic: 14.8 us -> none  [the longest x32 10.4 us: advance(): projected = jnp.sum(column * current, axis=1, keepdims=True)]
    reduce_scatter x1 -> x0, waiting for transfers between devices: 13.7 us -> none  [on_device(): lax.psum_scatter(jnp.einsum('tc,dc->td', cot_rows, weight_in, preferred_e...]
    unnamed x41 -> x7, local copies, waits for them, and re-layouts: 18.9 us -> 9.22 us
  transfers between devices with their start and end apart: 5 -> 0, of which waited for: 4 -> 0; matrix products, arithmetic and copies ran while one was open for 9% -> 0% of each run, Pallas kernels for 0% -> 0%
where the time goes in v1:
time: 124 us; the launch traced here: 123 us
  Pallas kernels  107 us (86%)
  local copies, waits for them, and re-layouts  15.6 us (13%)
    pallas_call x1, Pallas kernels, on_device(): pl.pallas_call(kernel, out_shape=(jax.ShapeDtypeStruct((SHARE, D), BF16),...  107 us
    unnamed x7, local copies, waits for them, and re-layouts  9.22 us
    pallas_call x4, local copies, waits for them, and re-layouts, on_device(): pl.pallas_call(kernel, out_shape=(jax.ShapeDtypeStruct((SHARE, D), BF16),...  6.43 us

profile of v1, /device:TPU:1, one launch (start us, length us, event | category | flops | bytes accessed | tf_op | source)
XLA Modules:
  0.0 123.2 jit_solution(15754760599562286891)
XLA Ops:
  0.6 1.5 %copy.19.narrow_start = f32[2,128,32]{2,1,0:T(8,128)} copy(f32[2,128,32]{1,2,0:T(8,128)} %param.21) | data formatting | bytes 65536 | tf_op args[10]
  2.1 1.7 %copy.18.wide_start = f32[2,256,32]{2,1,0:T(8,128)} copy(f32[2,256,32]{1,2,0:T(8,128)} %param.20) | data formatting | bytes 131072 | tf_op args[9]
  3.8 106.9 %shard_map.162 = (bf16[64,2304]{1,0:T(8,128)(2,1)}, f32[2,1,72,32]{3,2,1,0:T(8,128)}, f32[2,1,72,32]{3,2,1,0:T(8,128)}, f32[2,256,32]{2,1,0:T(8,128)}, f32[2,128...) custom-call(bf16[64,2304]{1,0:T(8,128)(2,1)} %x_in.1, ...), custom_call_target="tpu_custom_call" | custom-call | tf_op jit(solution)/shard_map/pallas_call | solution.py:498
  110.7 1.6 %copy.20 = f32[2,1,72,32]{2,3,1,0:T(8,128)} copy(f32[2,1,72,32]{3,2,1,0:T(8,128)} %get-tuple-element.8) | data formatting | bytes 36864 | tf_op jit(solution)/shard_map/pallas_call | solution.py:498
  112.3 1.6 %copy.21 = f32[2,1,72,32]{2,3,1,0:T(8,128)} copy(f32[2,1,72,32]{3,2,1,0:T(8,128)} %get-tuple-element.9) | data formatting | bytes 36864 | tf_op jit(solution)/shard_map/pallas_call | solution.py:498
  113.9 1.6 %copy.23 = f32[2,128,32]{1,2,0:T(8,128)} copy(f32[2,128,32]{2,1,0:T(8,128)} %get-tuple-element.11) | data formatting | bytes 65536 | tf_op jit(solution)/shard_map/pallas_call | solution.py:498
  115.5 1.7 %copy.22 = f32[2,256,32]{1,2,0:T(8,128)} copy(f32[2,256,32]{2,1,0:T(8,128)} %get-tuple-element.10) | data formatting | bytes 131072 | tf_op jit(solution)/shard_map/pallas_call | solution.py:498
  117.2 1.7 %copy.27 = bf16[64,2304]{1,0:T(8,128)(2,1)} copy(bf16[64,2304]{1,0:T(8,128)(2,1)} %get-tuple-element.21) | data formatting | bytes 589824
  118.9 0.0 copy-start
  118.9 3.3 %copy.28 = bf16[1,2,2304,256]{3,2,1,0:T(8,128)(2,1)} copy(bf16[1,2,2304,256]{3,2,1,0:T(8,128)(2,1)} %get-tuple-element.26) | data formatting | bytes 4718592
  122.2 0.0 copy-done
  122.2 1.0 copy.29
Async XLA Ops:
  118.9 3.3 %copy-start = (bf16[1,2,2304,128]{3,2,1,0:T(8,128)(2,1)S(1)}, bf16[1,2,2304,128]{3,2,1,0:T(8,128)(2,1)}, u32[]{:S(2)}) copy-start(bf16[1,2,2304,128]{3,2,1,0:T(8,128)(2,1)} %get-tuple-element.27) | copy-start | bytes 3538948

commit v2 on v1

v2 whole, which is shorter than its diff:
```python
import jax
import jax.numpy as jnp
from jax import lax
from jax.experimental import pallas as pl
from jax.experimental.pallas import tpu as pltpu
from jax.sharding import PartitionSpec as P

MESH = pl.DeviceIdType.MESH
F32 = jnp.float32
BF16 = jnp.bfloat16

D = 2304
HALF = D // 2
TOK = 512
SHARE = 64
PART = SHARE // 2
FINE = SHARE // 4
RANK = 32
N_DP = 32
N_MP = 8
CHIPS = N_DP // 2
REDUCERS = 12
ROWS_P = D // N_DP
COLS = ((0, 256), (256, 128), (384, 128), (512, 256))
INTO = 512
ALL = 768


def split(value):
    high = value.astype(BF16)
    return high, (value - high.astype(F32)).astype(BF16)


def dot(a, b, on_a=1, on_b=0):
    return lax.dot_general(a, b, (((on_a,), (on_b,)), ((), ())), preferred_element_type=F32)


def kernel(
    x_in, out_grad, context, query_grad, keyval_grad, query_weight, keyval_weight,
    wide_error, narrow_error, wide_start, narrow_start,
    input_grad, wide_p, narrow_p, wide_q, narrow_q, wide_new, narrow_new,
    xf, yf, gv, wv, ev, sw, sn, st, tx, ty, pg, rr, sh, sl,
    fl, ra, rbx, rby, ff, rowbuf, pb, pt, pc, ql, rq, ry, qf, qbd,
    load_sem, x_send, x_recv, y_send, y_recv, z_send, z_recv,
    a_send, a_recv, b_send, b_recv, c_send, c_recv, d_send, d_recv,
    e_send, e_recv, f_send, f_recv, h_send, h_recv,
):
    dp = lax.axis_index("dp")
    mp = lax.axis_index("mp")
    core = dp % 2
    chip = dp // 2
    mate = dp + 1 - 2 * core
    ring = ((mp + 1) % N_MP, (mp + N_MP - 1) % N_MP)

    def along(way, steps):
        return (mp + steps) % N_MP if way == 0 else (mp + N_MP - steps) % N_MP

    loads = [
        (query_grad, gv.at[:, 0:256]),
        (keyval_grad.at[0], gv.at[:, 256:384]),
        (keyval_grad.at[1], gv.at[:, 384:512]),
        (query_weight, wv.at[:, 0:256]),
        (keyval_weight.at[0], wv.at[:, 256:384]),
        (keyval_weight.at[1], wv.at[:, 384:512]),
        (wide_start, sw),
        (narrow_start, sn),
        (wide_error.at[0, 0], ev.at[:, 0:256]),
        (narrow_error.at[0, 0], ev.at[:, 256:384]),
        (narrow_error.at[0, 1], ev.at[:, 384:512]),
        (wide_error.at[0, 1], ev.at[:, 512:768]),
        (context, gv.at[:, 512:768]),
        (x_in, xf.at[pl.ds(pl.multiple_of(mp * SHARE, SHARE), SHARE), :]),
        (out_grad, yf.at[pl.ds(pl.multiple_of(mp * SHARE, SHARE), SHARE), :]),
    ]
    loads = [pltpu.make_async_copy(a, b, load_sem.at[i]) for i, (a, b) in enumerate(loads)]
    for copy in loads:
        copy.start()

    barrier = pltpu.get_barrier_semaphore()
    for way in (0, 1):
        pl.semaphore_signal(barrier, inc=1, device_id=(dp, ring[way]), device_id_type=MESH)

    @pl.loop(1, N_DP)
    def _(k):
        pl.semaphore_signal(barrier, inc=1, device_id=((dp + k) % N_DP, mp), device_id_type=MESH)

    pl.semaphore_wait(barrier, N_DP + 1)

    def hop(own, full, send, recv, way, step, role):
        part = role if way == 0 else 3 - role
        owner = along(1 - way, step - 1)
        rows = pl.ds(pl.multiple_of(owner * SHARE + part * FINE, FINE), FINE)
        src = own.at[part * FINE:(part + 1) * FINE, :] if step == 1 else full.at[rows, :]
        return pltpu.make_async_remote_copy(
            src_ref=src, dst_ref=full.at[rows, :],
            send_sem=send.at[way, step - 1, role], recv_sem=recv.at[way, step - 1, role],
            device_id=(dp, ring[way]), device_id_type=MESH,
        )

    def x_hop(way, step, role):
        return hop(x_in, xf, x_send, x_recv, way, step, role)

    def y_hop(way, step, role):
        return hop(out_grad, yf, y_send, y_recv, way, step, role)

    def first(make, roles=(0, 1, 2, 3)):
        for role in roles:
            for way in (0, 1):
                make(way, 1, role).start()

    def forward(make, step, *roles):
        for role in roles:
            for way in (0, 1):
                make(way, step - 1, role).wait_recv()
                make(way, step, role).start()

    def finish_ring(make):
        for step, role in ((3, 2), (3, 3), (4, 0), (4, 1)):
            for way in (0, 1):
                make(way, step, role).wait_recv()

    def drain_ring(make):
        for way in (0, 1):
            for step in (1, 2, 3, 4):
                for role in (0, 1, 2, 3):
                    if step < 4 or role < 2:
                        make(way, step, role).wait_send()

    def z_hop(way, step, role):
        part = way if role == 0 else 1 - way
        dest = along(way, 5 - step)
        rows = pl.ds(pl.multiple_of(dest * SHARE + part * PART, PART), PART)
        here = slice(part * PART, (part + 1) * PART)
        if step == (1 if role == 0 else 2):
            src = pg.at[rows, :]
        else:
            src = rr.at[way, step - 2, here, :]
        return pltpu.make_async_remote_copy(
            src_ref=src, dst_ref=rr.at[way, step - 1, here, :],
            send_sem=z_send.at[way, step - 1, role], recv_sem=z_recv.at[way, step - 1, role],
            device_id=(dp, ring[way]), device_id_type=MESH,
        ), rows, here

    def z_first():
        for way in (0, 1):
            z_hop(way, 1, 0)[0].start()
        for way in (0, 1):
            z_hop(way, 2, 1)[0].start()

    def z_step(step, role):
        for way in (0, 1):
            z_hop(way, step - 1, role)[0].wait_recv()
            copy, rows, here = z_hop(way, step, role)
            rr[way, step - 2, here, :] += pg[rows, :]
            copy.start()

    x_rows = slice(0, 96)
    y_rows = slice(96, 128)

    def chunk(group, p):
        if group == 0:
            return pl.ds(pl.multiple_of(p * 8, 8), 8), pl.ds(0, HALF)
        return (
            pl.ds(pl.multiple_of(96 + (p // 3) * 8, 8), 8),
            pl.ds(pl.multiple_of((p % 3) * 384, 384), 384),
        )

    def a_copy(group):
        rows = (x_rows, y_rows)[group]
        return pltpu.make_async_remote_copy(
            src_ref=fl.at[1 - core, rows], dst_ref=ra.at[rows],
            send_sem=a_send.at[group], recv_sem=a_recv.at[group],
            device_id=(mate, mp), device_id_type=MESH,
        )

    def b_copy(group, k, other):
        rows, lanes = chunk(group, other)
        return pltpu.make_async_remote_copy(
            src_ref=fl.at[core, rows, lanes], dst_ref=(rbx, rby)[group].at[k - 1],
            send_sem=b_send.at[group, k - 1], recv_sem=b_recv.at[group, k - 1],
            device_id=(2 * other + core, mp), device_id_type=MESH,
        )

    def c_copy(group, k, other, source):
        rows, lanes = chunk(group, source)
        own = ff.at[core, rows, lanes]
        return pltpu.make_async_remote_copy(
            src_ref=own, dst_ref=own,
            send_sem=c_send.at[group, k - 1], recv_sem=c_recv.at[group, k - 1],
            device_id=(2 * other + core, mp), device_id_type=MESH,
        )

    def d_copy(group):
        own = ff.at[core, (x_rows, y_rows)[group]]
        return pltpu.make_async_remote_copy(
            src_ref=own, dst_ref=own, send_sem=d_send.at[group], recv_sem=d_recv.at[group],
            device_id=(mate, mp), device_id_type=MESH,
        )

    def to_reducers(group):
        rows = (x_rows, y_rows)[group]
        a_copy(group).wait_recv()
        fl[core, rows] += ra[rows]

        @pl.loop(1, CHIPS)
        def _(k):
            other = (chip + k) % CHIPS

            @pl.when(other < REDUCERS)
            def _():
                b_copy(group, k, other).start()

    def from_reducers(group):
        @pl.when(chip < REDUCERS)
        def _():
            @pl.loop(1, CHIPS)
            def _(k):
                b_copy(group, k, chip).wait_recv()

            rows, lanes = chunk(group, chip)
            ff[core, rows, lanes] = fl[core, rows, lanes] + jnp.sum((rbx, rby)[group][...], axis=0)

            @pl.loop(1, CHIPS)
            def _(k):
                c_copy(group, k, (chip + k) % CHIPS, chip).start()

    def to_mate(group):
        @pl.loop(1, CHIPS)
        def _(k):
            source = (chip + CHIPS - k) % CHIPS

            @pl.when(source < REDUCERS)
            def _():
                c_copy(group, k, chip, source).wait_recv()

        d_copy(group).start()

    def from_mate(group):
        a_copy(group).wait_send()

        @pl.loop(1, CHIPS)
        def _(k):
            other = (chip + k) % CHIPS

            @pl.when(other < REDUCERS)
            def _():
                b_copy(group, k, other).wait_send()

        @pl.when(chip < REDUCERS)
        def _():
            @pl.loop(1, CHIPS)
            def _(k):
                c_copy(group, k, (chip + k) % CHIPS, chip).wait_send()

        d_copy(group).wait()

    first(x_hop)
    for i in range(6):
        loads[i].wait()

    def partial_input_grad(start, stop):
        @pl.loop(start, stop)
        def _(j):
            cols = pl.ds(pl.multiple_of(j * 256, 256), 256)
            pg[:, cols] = dot(gv[:, 0:INTO], wv[cols, :], 1, 1)

    partial_input_grad(0, 3)
    forward(x_hop, 2, 0, 1)
    partial_input_grad(3, 6)
    forward(x_hop, 2, 2, 3)
    partial_input_grad(6, 9)
    forward(x_hop, 3, 0)

    for i in (6, 7):
        loads[i].wait()
    for b, (at, width) in enumerate(COLS):
        high, low = split(sw[0 if b == 0 else 1] if width == 256 else sn[b - 1])
        st[0:RANK, at:at + width] = high
        st[RANK:2 * RANK, at:at + width] = low
    loads[12].wait()
    for b, (at, width) in enumerate(COLS):
        t = dot(st[:, at:at + width], gv[:, at:at + width], 1, 1)
        high, low = split(t[:RANK] + t[RANK:])
        if b < 3:
            tx[b * RANK:(b + 1) * RANK, :] = high
            tx[96 + b * RANK:96 + (b + 1) * RANK, :] = low
        else:
            ty[0:RANK, :] = high
            ty[RANK:2 * RANK, :] = low
    qbd[...] = jnp.zeros_like(qbd)

    forward(x_hop, 3, 1)
    for i in (8, 9, 10, 11):
        loads[i].wait()

    def error_factors(start, stop):
        @pl.loop(start, stop)
        def _(j):
            rows = pl.ds(pl.multiple_of(j * 384, 384), 384)
            lanes = pl.ds(pl.multiple_of((j % 3) * 384, 384), 384)
            for b, (at, width) in enumerate(COLS):
                e = dot(st[:, at:at + width], ev[rows, at:at + width], 1, 1)
                fl[j // 3, b * RANK:(b + 1) * RANK, lanes] = e[:RANK] + e[RANK:]

    error_factors(0, 3)
    forward(x_hop, 3, 2)
    error_factors(3, 6)
    forward(x_hop, 3, 3)
    forward(x_hop, 4, 0, 1)
    first(y_hop)
    loads[13].wait()
    finish_ring(x_hop)

    @pl.loop(0, 6)
    def _(j):
        cols = pl.ds(pl.multiple_of(j * 384, 384), 384)
        lanes = pl.ds(pl.multiple_of((j % 3) * 384, 384), 384)
        f = dot(tx[...], xf[:, cols])
        fl[j // 3, 0:96, lanes] += f[:96] + f[96:]

    a_copy(0).start()

    def sums_into(start, stop):
        @pl.loop(start, stop)
        def _(j):
            rows = pl.ds(pl.multiple_of(j * 256, 256), 256)
            total = dot(xf[:, rows], gv[:, 0:INTO], 0, 0) + ev[rows, 0:INTO].astype(F32)
            high, low = split(total)
            sh[rows, 0:INTO] = high
            sl[rows, 0:INTO] = low

    forward(y_hop, 2, 0, 1)
    to_reducers(0)
    forward(y_hop, 2, 2, 3)
    sums_into(0, 3)
    forward(y_hop, 3, 0, 1)
    from_reducers(0)
    sums_into(3, 6)
    forward(y_hop, 3, 2)
    sums_into(6, 9)
    forward(y_hop, 3, 3)
    to_mate(0)
    forward(y_hop, 4, 0, 1)
    z_first()
    loads[14].wait()
    from_mate(0)
    finish_ring(y_hop)

    @pl.loop(0, 6)
    def _(j):
        cols = pl.ds(pl.multiple_of(j * 384, 384), 384)
        lanes = pl.ds(pl.multiple_of((j % 3) * 384, 384), 384)
        f = dot(ty[...], yf[:, cols])
        fl[j // 3, 96:128, lanes] += f[:RANK] + f[RANK:]

    a_copy(1).start()

    def gram_schmidt(block, which):
        @pl.loop(0, 8)
        def _(i):
            norms = {}
            for b in which:
                row = [ff[h, pl.ds(b * RANK + block * 8 + i, 1), :] for h in (0, 1)]
                for h in (0, 1):
                    rowbuf[h, b * 8:b * 8 + 8, :] = jnp.broadcast_to(row[h], (8, HALF))
                norms[b] = jnp.sum(row[0] * row[0] + row[1] * row[1], axis=1, keepdims=True)
            later = lax.broadcasted_iota(jnp.int32, (8, 1), 0) > i
            scales = {}
            for b in which:
                for t in range(block, 4):
                    at = slice(b * RANK + t * 8, b * RANK + t * 8 + 8)
                    r = slice(b * 8, b * 8 + 8)
                    dots = jnp.sum(
                        ff[0, at, :] * rowbuf[0, r, :] + ff[1, at, :] * rowbuf[1, r, :],
                        axis=1, keepdims=True,
                    )
                    scale = dots / norms[b]
                    scales[b, t] = jnp.where(later, scale, 0.0) if t == block else scale
            for b in which:
                for t in range(block, 4):
                    at = slice(b * RANK + t * 8, b * RANK + t * 8 + 8)
                    for h in (0, 1):
                        ff[h, at, :] -= scales[b, t] * rowbuf[h, b * 8:b * 8 + 8, :]

    def right_factors(which):
        for b in which:
            at = slice(b * RANK, (b + 1) * RANK)
            squares = jnp.sum(
                ff[0, at, :] * ff[0, at, :] + ff[1, at, :] * ff[1, at, :], axis=1, keepdims=True
            )
            size = jnp.sqrt(squares)
            for h in (0, 1):
                unit = ff[h, at, :] / size
                ff[h, at, :] = unit
                high, low = split(unit)
                pb[2 * b * RANK:(2 * b + 1) * RANK, h * HALF:(h + 1) * HALF] = high
                pb[(2 * b + 1) * RANK:(2 * b + 2) * RANK, h * HALF:(h + 1) * HALF] = low
        for b in which:
            at, width = COLS[b]
            both = dot(pb[2 * b * RANK:(2 * b + 2) * RANK, :], sh[:, at:at + width])
            rest = dot(pb[2 * b * RANK:(2 * b + 1) * RANK, :], sl[:, at:at + width])
            ql[:, at:at + width] = both[:RANK] + both[RANK:] + rest

    into = (0, 1, 2)
    outof = (3,)

    @pl.loop(0, 9)
    def _(j):
        rows = pl.ds(pl.multiple_of(j * 256, 256), 256)
        total = dot(yf[:, rows], gv[:, INTO:ALL], 0, 0) + ev[rows, INTO:ALL].astype(F32)
        high, low = split(total)
        sh[rows, INTO:ALL] = high
        sl[rows, INTO:ALL] = low

    to_reducers(1)
    z_step(2, 0)
    gram_schmidt(0, into)
    from_reducers(1)
    gram_schmidt(1, into)
    z_step(3, 1)
    gram_schmidt(2, into)
    gram_schmidt(3, into)
    to_mate(1)
    right_factors(into)
    from_mate(1)
    z_step(3, 0)
    gram_schmidt(0, outof)
    gram_schmidt(1, outof)
    gram_schmidt(2, outof)
    gram_schmidt(3, outof)
    right_factors(outof)

    place = dp % 8
    line = dp // 8

    def part_of(j):
        return (
            pl.ds(pl.multiple_of((j % 4) * 8, 8), 8),
            pl.ds(pl.multiple_of((j // 4) * 384, 384), 384),
        )

    own_part = part_of(place)

    def e_copy(k):
        other = (place + k) % 8
        rows, lanes = part_of(other)
        return pltpu.make_async_remote_copy(
            src_ref=ql.at[rows, lanes], dst_ref=rq.at[k - 1],
            send_sem=e_send.at[k - 1], recv_sem=e_recv.at[k - 1],
            device_id=(line * 8 + other, mp), device_id_type=MESH,
        )

    def f_copy(k):
        return pltpu.make_async_remote_copy(
            src_ref=ry.at[line], dst_ref=ry.at[line],
            send_sem=f_send.at[k - 1], recv_sem=f_recv.at[k - 1],
            device_id=(((line + k) % 4) * 8 + place, mp), device_id_type=MESH,
        )

    def h_copy(k):
        own = qf.at[own_part[0], own_part[1]]
        return pltpu.make_async_remote_copy(
            src_ref=own, dst_ref=own,
            send_sem=h_send.at[k - 1], recv_sem=h_recv.at[k - 1],
            device_id=(line * 8 + (place + k) % 8, mp), device_id_type=MESH,
        )

    @pl.loop(1, 8)
    def _(k):
        e_copy(k).start()

    for h in (0, 1):
        @pl.loop(0, 3)
        def _(j):
            lanes = pl.ds(pl.multiple_of(j * 384, 384), 384)
            rows = pl.ds(pl.multiple_of(h * HALF + j * 384, 384), 384)
            by_row = jnp.transpose(ff[h, :, lanes])
            pt[rows, :] = by_row
            high, low = split(by_row)
            pc[rows, 0:128] = high
            pc[rows, 128:256] = high
            pc[rows, 256:384] = low

    @pl.loop(1, 8)
    def _(k):
        e_copy(k).wait_recv()

    ry[line] = ql[own_part[0], own_part[1]] + jnp.sum(rq[...], axis=0)

    @pl.loop(1, 4)
    def _(k):
        f_copy(k).start()

    z_step(4, 1)

    @pl.loop(1, 4)
    def _(k):
        f_copy(k).wait_recv()

    qf[own_part[0], own_part[1]] = (ry[0] + ry[1] + ry[2] + ry[3]) * (1.0 / N_DP)

    @pl.loop(1, 8)
    def _(k):
        h_copy(k).start()

    mine = jnp.transpose(pt[pl.ds(pl.multiple_of(dp * ROWS_P, 8), ROWS_P), :])
    for b, ref in enumerate((wide_p.at[0], narrow_p.at[0], narrow_p.at[1], wide_p.at[1])):
        ref[0] = mine[b * RANK:(b + 1) * RANK]

    @pl.loop(1, 8)
    def _(k):
        h_copy(k).wait_recv()

    for b, (at, width) in enumerate(COLS):
        q = qf[:, at:at + width]
        (wide_q, narrow_q)[width == 128][(0, 0, 1, 1)[b]] = q
        high, low = split(q)
        qbd[b * RANK:(b + 1) * RANK, at:at + width] = high
        qbd[128 + b * RANK:128 + (b + 1) * RANK, at:at + width] = low
        qbd[256 + b * RANK:256 + (b + 1) * RANK, at:at + width] = high

    z_step(4, 0)

    @pl.loop(0, 9)
    def _(j):
        rows = pl.ds(pl.multiple_of(j * 256, 256), 256)
        low_rank = dot(pc[rows, :], qbd[...])
        new = (sh[rows, :].astype(F32) + sl[rows, :].astype(F32) - low_rank).astype(BF16)
        for b, ref in enumerate((wide_new, narrow_new, narrow_new, wide_new)):
            at, width = COLS[b]
            ref[0, (0, 0, 1, 1)[b], rows, :] = new[:, at:at + width]

    for way in (0, 1):
        for role in (0, 1):
            z_hop(way, 4, role)[0].wait_recv()
    own = pl.ds(pl.multiple_of(mp * SHARE, SHARE), SHARE)
    input_grad[...] = (pg[own, :] + rr[0, 3] + rr[1, 3]).astype(BF16)

    drain_ring(x_hop)
    drain_ring(y_hop)
    for way in (0, 1):
        for step in (1, 2, 3, 4):
            for role in (0, 1):
                if (step, role) != (1, 1):
                    z_hop(way, step, role)[0].wait_send()

    @pl.loop(1, 8)
    def _(k):
        e_copy(k).wait_send()
        h_copy(k).wait_send()

    @pl.loop(1, 4)
    def _(k):
        f_copy(k).wait_send()


def hand_out(*refs):
    sources, targets, sem = refs[:7], refs[7:14], refs[14]
    copies = [pltpu.make_async_copy(a, b, sem.at[i]) for i, (a, b) in enumerate(zip(sources, targets))]
    for copy in copies:
        copy.start()
    for copy in copies:
        copy.wait()


def on_device(*args):
    sems = pltpu.SemaphoreType.DMA
    vmem = pltpu.VMEM
    args = args[:9] + tuple(jnp.swapaxes(a, 1, 2) for a in args[9:])
    shapes = (
        ((SHARE, D), BF16),
        ((2, 1, RANK, ROWS_P), F32),
        ((2, 1, RANK, ROWS_P), F32),
        ((2, RANK, 256), F32),
        ((2, RANK, 128), F32),
        ((1, 2, D, 256), BF16),
        ((1, 2, D, 128), BF16),
    )
    outs = pl.pallas_call(
        kernel,
        out_shape=tuple(pltpu.VMEM(shape, dtype) for shape, dtype in shapes),
        in_specs=[pl.BlockSpec(memory_space=pltpu.HBM)] * 11,
        out_specs=tuple([pl.BlockSpec(memory_space=pltpu.VMEM)] * 7),
        scratch_shapes=[
            vmem((TOK, D), BF16),
            vmem((TOK, D), BF16),
            vmem((TOK, ALL), BF16),
            vmem((D, INTO), BF16),
            vmem((D, ALL), BF16),
            vmem((2, RANK, 256), F32),
            vmem((2, RANK, 128), F32),
            vmem((2 * RANK, ALL), BF16),
            vmem((192, TOK), BF16),
            vmem((64, TOK), BF16),
            vmem((TOK, D), F32),
            vmem((2, 4, SHARE, D), F32),
            vmem((D, ALL), BF16),
            vmem((D, ALL), BF16),
            vmem((2, 128, HALF), F32),
            vmem((128, HALF), F32),
            vmem((CHIPS - 1, 8, HALF), F32),
            vmem((CHIPS - 1, 8, 384), F32),
            vmem((2, 128, HALF), F32),
            vmem((2, 32, HALF), F32),
            vmem((256, D), BF16),
            vmem((D, 128), F32),
            vmem((D, 384), BF16),
            vmem((RANK, ALL), F32),
            vmem((7, 8, 384), F32),
            vmem((4, 8, 384), F32),
            vmem((RANK, ALL), F32),
            vmem((384, ALL), BF16),
            sems((15,)),
            sems((2, 4, 4)), sems((2, 4, 4)),
            sems((2, 4, 4)), sems((2, 4, 4)),
            sems((2, 4, 2)), sems((2, 4, 2)),
            sems((2,)), sems((2,)),
            sems((2, CHIPS - 1)), sems((2, CHIPS - 1)),
            sems((2, CHIPS - 1)), sems((2, CHIPS - 1)),
            sems((2,)), sems((2,)),
            sems((7,)), sems((7,)),
            sems((3,)), sems((3,)),
            sems((7,)), sems((7,)),
        ],
        compiler_params=pltpu.CompilerParams(
            collective_id=0, has_side_effects=True, vmem_limit_bytes=59 * 1024 * 1024
        ),
    )(*args)
    outs = pl.pallas_call(
        hand_out,
        out_shape=tuple(jax.ShapeDtypeStruct(shape, dtype) for shape, dtype in shapes),
        in_specs=[pl.BlockSpec(memory_space=pltpu.VMEM)] * 7,
        out_specs=tuple([pl.BlockSpec(memory_space=pl.ANY)] * 7),
        scratch_shapes=[sems((7,))],
        compiler_params=pltpu.CompilerParams(vmem_limit_bytes=16 * 1024 * 1024),
    )(*outs)
    turned = [jnp.swapaxes(a, -1, -2) for a in outs[1:5]]
    return (outs[0], *turned, *outs[5:])


def solution(mesh):
    return jax.shard_map(
        on_device,
        mesh=mesh,
        in_specs=(
            P(("dp", "mp"), None),
            P(("dp", "mp"), None),
            P("dp", "mp"),
            P("dp", "mp"),
            P(None, "dp", "mp"),
            P(None, "mp"),
            P(None, None, "mp"),
            P("dp", None, None, "mp"),
            P("dp", None, None, "mp"),
            P(None, "mp", None),
            P(None, "mp", None),
        ),
        out_specs=(
            P(("dp", "mp"), None),
            P(None, "mp", "dp", None),
            P(None, "mp", "dp", None),
            P(None, "mp", None),
            P(None, "mp", None),
            P("dp", None, None, "mp"),
            P("dp", None, None, "mp"),
        ),
        check_vma=False,
    )
```

time: 124 us -> 113 us (0.911)
  local copies, waits for them, and re-layouts: 15.6 us -> 0 us
  Pallas kernels: 107 us -> 113 us
    unnamed x7 -> x0, local copies, waits for them, and re-layouts: 9.22 us -> none
    pallas_call x4 -> x0, local copies, waits for them, and re-layouts: 6.43 us -> none  [on_device(): pl.pallas_call(kernel, out_shape=(jax.ShapeDtypeStruct((SHARE, D), BF16),...]
    pallas_call x1 -> x2, Pallas kernels: 107 us -> 113 us  [the longest x1 111 us: on_device(): pl.pallas_call(kernel, out_shape=tuple((pltpu.VMEM(shape, dtype) for shap...]
where the time goes in v2:
time: 113 us
  Pallas kernels  113 us (100%)
    pallas_call x1, Pallas kernels, on_device(): pl.pallas_call(kernel, out_shape=tuple((pltpu.VMEM(shape, dtype) for shap...  111 us

profile of v2, /device:TPU:1, one launch (start us, length us, event | category | flops | bytes accessed | tf_op | source)
XLA Modules:
  0.0 113.2 jit_solution(2774159665159298907)
XLA Ops:
  0.6 110.6 %shard_map.162 = (bf16[64,2304]{1,0:T(8,128)(2,1)S(1)}, f32[2,1,32,72]{3,2,1,0:T(8,128)S(1)}, f32[2,1,32,72]{3,2,1,0:T(8,128)S(1)}, f32[2,32,256]{2,1,0:T(8,128)...) custom-call(bf16[64,2304]{1,0:T(8,128)(2,1)} %x_in.1, ...), custom_call_target="tpu_custom_call" | custom-call | tf_op jit(solution)/shard_map/pallas_call | solution.py:579
  111.2 2.0 %shard_map.163 = (bf16[64,2304]{1,0:T(8,128)(2,1)}, f32[2,1,32,72]{3,2,1,0:T(8,128)}, f32[2,1,32,72]{3,2,1,0:T(8,128)}, f32[2,32,256]{2,1,0:T(8,128)}, f32[2,32,...) custom-call(bf16[64,2304]{1,0:T(8,128)(2,1)S(1)} %get-tuple-element.21.refs_0_, ...), custom_call_target="tpu_custom_call" | custom-call | tf_op jit(solution)/shard_map/pallas_call | solution.py:629

commit v3 on v2

--- a/solution.py
+++ b/solution.py
@@ -73,18 +73,24 @@
         (out_grad, yf.at[pl.ds(pl.multiple_of(mp * SHARE, SHARE), SHARE), :]),
     ]
     loads = [pltpu.make_async_copy(a, b, load_sem.at[i]) for i, (a, b) in enumerate(loads)]
-    for copy in loads:
-        copy.start()
+    for i in range(6):
+        loads[i].start()
 
     barrier = pltpu.get_barrier_semaphore()
     for way in (0, 1):
         pl.semaphore_signal(barrier, inc=1, device_id=(dp, ring[way]), device_id_type=MESH)
 
-    @pl.loop(1, N_DP)
-    def _(k):
-        pl.semaphore_signal(barrier, inc=1, device_id=((dp + k) % N_DP, mp), device_id_type=MESH)
-
-    pl.semaphore_wait(barrier, N_DP + 1)
+    @pl.loop(1, CHIPS)
+    def _(k):
+        other = 2 * ((chip + k) % CHIPS) + core
+        pl.semaphore_signal(barrier, inc=1, device_id=(other, mp), device_id_type=MESH)
+
+    @pl.loop(0, 4)
+    def _(k):
+        other = (dp // 8) * 8 + 2 * k + 1 - core
+        pl.semaphore_signal(barrier, inc=1, device_id=(other, mp), device_id_type=MESH)
+
+    pl.semaphore_wait(barrier, 2 + (CHIPS - 1) + 4)
 
     def hop(own, full, send, recv, way, step, role):
         part = role if way == 0 else 3 - role
@@ -141,11 +147,9 @@
             device_id=(dp, ring[way]), device_id_type=MESH,
         ), rows, here
 
-    def z_first():
+    def z_first(step, role):
         for way in (0, 1):
-            z_hop(way, 1, 0)[0].start()
-        for way in (0, 1):
-            z_hop(way, 2, 1)[0].start()
+            z_hop(way, step, role)[0].start()
 
     def z_step(step, role):
         for way in (0, 1):
@@ -255,6 +259,8 @@
         d_copy(group).wait()
 
     first(x_hop)
+    for copy in loads[6:]:
+        copy.start()
     for i in range(6):
         loads[i].wait()
 
@@ -329,22 +335,20 @@
             sh[rows, 0:INTO] = high
             sl[rows, 0:INTO] = low
 
-    forward(y_hop, 2, 0, 1)
+    forward(y_hop, 2, 0, 1, 2)
+    forward(y_hop, 2, 3)
+    sums_into(0, 3)
     to_reducers(0)
-    forward(y_hop, 2, 2, 3)
-    sums_into(0, 3)
-    forward(y_hop, 3, 0, 1)
+    forward(y_hop, 3, 0)
+    sums_into(3, 6)
+    forward(y_hop, 3, 1)
+    sums_into(6, 9)
+    forward(y_hop, 3, 2, 3)
+    forward(y_hop, 4, 0, 1)
     from_reducers(0)
-    sums_into(3, 6)
-    forward(y_hop, 3, 2)
-    sums_into(6, 9)
-    forward(y_hop, 3, 3)
-    to_mate(0)
-    forward(y_hop, 4, 0, 1)
-    z_first()
     loads[14].wait()
-    from_mate(0)
     finish_ring(y_hop)
+    z_first(1, 0)
 
     @pl.loop(0, 6)
     def _(j):
@@ -354,6 +358,8 @@
         fl[j // 3, 96:128, lanes] += f[:RANK] + f[RANK:]
 
     a_copy(1).start()
+    z_first(2, 1)
+    to_mate(0)
 
     def gram_schmidt(block, which):
         @pl.loop(0, 8)
@@ -413,21 +419,22 @@
         sl[rows, INTO:ALL] = low
 
     to_reducers(1)
-    z_step(2, 0)
+    from_mate(0)
     gram_schmidt(0, into)
     from_reducers(1)
     gram_schmidt(1, into)
-    z_step(3, 1)
     gram_schmidt(2, into)
+    z_step(2, 0)
     gram_schmidt(3, into)
     to_mate(1)
     right_factors(into)
     from_mate(1)
-    z_step(3, 0)
+    z_step(3, 1)
     gram_schmidt(0, outof)
     gram_schmidt(1, outof)
     gram_schmidt(2, outof)
     gram_schmidt(3, outof)
+    z_step(3, 0)
     right_factors(outof)
 
     place = dp % 8
@@ -529,6 +536,7 @@
         for b, ref in enumerate((wide_new, narrow_new, narrow_new, wide_new)):
             at, width = COLS[b]
             ref[0, (0, 0, 1, 1)[b], rows, :] = new[:, at:at + width]
+
 
     for way in (0, 1):
         for role in (0, 1):

time: 113 us -> 107 us (0.947)
  Pallas kernels: 113 us -> 106 us
    pallas_call x1, Pallas kernels: 111 us -> 104 us  [on_device(): pl.pallas_call(kernel, out_shape=tuple((pltpu.VMEM(shape, dtype) for shap...]
where the time goes in v3:
time: 107 us
  Pallas kernels  106 us (99%)
    pallas_call x1, Pallas kernels, on_device(): pl.pallas_call(kernel, out_shape=tuple((pltpu.VMEM(shape, dtype) for shap...  104 us

profile of v3, /device:TPU:1, one launch (start us, length us, event | category | flops | bytes accessed | tf_op | source)
XLA Modules:
  0.0 107.1 jit_solution(4594811925728887143)
XLA Ops:
  0.6 104.4 %shard_map.162 = (bf16[64,2304]{1,0:T(8,128)(2,1)S(1)}, f32[2,1,32,72]{3,2,1,0:T(8,128)S(1)}, f32[2,1,32,72]{3,2,1,0:T(8,128)S(1)}, f32[2,32,256]{2,1,0:T(8,128)...) custom-call(bf16[64,2304]{1,0:T(8,128)(2,1)} %x_in.1, ...), custom_call_target="tpu_custom_call" | custom-call | tf_op jit(solution)/shard_map/pallas_call | solution.py:587
  105.1 2.0 %shard_map.163 = (bf16[64,2304]{1,0:T(8,128)(2,1)}, f32[2,1,32,72]{3,2,1,0:T(8,128)}, f32[2,1,32,72]{3,2,1,0:T(8,128)}, f32[2,32,256]{2,1,0:T(8,128)}, f32[2,32,...) custom-call(bf16[64,2304]{1,0:T(8,128)(2,1)S(1)} %get-tuple-element.21.refs_0_, ...), custom_call_target="tpu_custom_call" | custom-call | tf_op jit(solution)/shard_map/pallas_call | solution.py:637

commit v4 on v3

--- a/solution.py
+++ b/solution.py
@@ -23,6 +23,7 @@
 ROWS_P = D // N_DP
 COLS = ((0, 256), (256, 128), (384, 128), (512, 256))
 INTO = 512
+NEAR = 1792
 ALL = 768
 
 
@@ -40,8 +41,9 @@
     wide_error, narrow_error, wide_start, narrow_start,
     input_grad, wide_p, narrow_p, wide_q, narrow_q, wide_new, narrow_new,
     xf, yf, gv, wv, ev, sw, sn, st, tx, ty, pg, rr, sh, sl,
-    fl, ra, rbx, rby, ff, rowbuf, pb, pt, pc, ql, rq, ry, qf, qbd,
+    wn, cn, fl, ra, rbx, rby, ff, rowbuf, pb, pt, pc, ql, rq, ry, qf, qbd,
     load_sem, x_send, x_recv, y_send, y_recv, z_send, z_recv,
+    n_send, n_recv, p_send, p_recv, m_send, m_recv,
     a_send, a_recv, b_send, b_recv, c_send, c_recv, d_send, d_recv,
     e_send, e_recv, f_send, f_recv, h_send, h_recv,
 ):
@@ -137,12 +139,14 @@
         dest = along(way, 5 - step)
         rows = pl.ds(pl.multiple_of(dest * SHARE + part * PART, PART), PART)
         here = slice(part * PART, (part + 1) * PART)
-        if step == (1 if role == 0 else 2):
-            src = pg.at[rows, :]
+        if step == 1 + role:
+            src = pg.at[rows, NEAR:]
+            dst = rr.at[way, step - 1, here, NEAR:]
         else:
             src = rr.at[way, step - 2, here, :]
-        return pltpu.make_async_remote_copy(
-            src_ref=src, dst_ref=rr.at[way, step - 1, here, :],
+            dst = rr.at[way, step - 1, here, :]
+        return pltpu.make_async_remote_copy(
+            src_ref=src, dst_ref=dst,
             send_sem=z_send.at[way, step - 1, role], recv_sem=z_recv.at[way, step - 1, role],
             device_id=(dp, ring[way]), device_id_type=MESH,
         ), rows, here
@@ -155,7 +159,11 @@
         for way in (0, 1):
             z_hop(way, step - 1, role)[0].wait_recv()
             copy, rows, here = z_hop(way, step, role)
-            rr[way, step - 2, here, :] += pg[rows, :]
+            if step == 2 + role:
+                rr[way, step - 2, here, NEAR:] += pg[rows, NEAR:]
+                rr[way, step - 2, here, :NEAR] = pg[rows, :NEAR]
+            else:
+                rr[way, step - 2, here, :] += pg[rows, :]
             copy.start()
 
     x_rows = slice(0, 96)
@@ -258,11 +266,102 @@
 
         d_copy(group).wait()
 
+    rows_each = NEAR // CHIPS
+    half = pl.ds(pl.multiple_of(core * 256, 256), 256)
+    share = pl.ds(pl.multiple_of(chip * rows_each, rows_each), rows_each)
+
+    def feature_copy(way, role):
+        part = way if role == 0 else 1 - way
+        dest = along(way, 4 - role)
+        rows = pl.ds(pl.multiple_of(dest * SHARE + part * PART, PART), PART)
+        return pltpu.make_async_remote_copy(
+            src_ref=gv.at[rows, 0:INTO], dst_ref=cn.at[way, role * PART:(role + 1) * PART, :],
+            send_sem=n_send.at[way, role], recv_sem=n_recv.at[way, role],
+            device_id=(dp, ring[way]), device_id_type=MESH,
+        )
+
+    def weight_copy(way):
+        return pltpu.make_async_remote_copy(
+            src_ref=wv.at[share, half], dst_ref=wn.at[way, share, half],
+            send_sem=n_send.at[way, 2], recv_sem=n_recv.at[way, 2],
+            device_id=(dp, ring[way]), device_id_type=MESH,
+        )
+
+    def plane_copy(way, k):
+        own = wn.at[way, share, half]
+        return pltpu.make_async_remote_copy(
+            src_ref=own, dst_ref=own,
+            send_sem=p_send.at[way, k - 1], recv_sem=p_recv.at[way, k - 1],
+            device_id=(2 * ((chip + k) % CHIPS) + core, mp), device_id_type=MESH,
+        )
+
+    def mate_copy(way):
+        own = wn.at[way, :, half]
+        return pltpu.make_async_remote_copy(
+            src_ref=own, dst_ref=own, send_sem=m_send.at[way], recv_sem=m_recv.at[way],
+            device_id=(mate, mp), device_id_type=MESH,
+        )
+
+    def to_neighbours():
+        for way in (0, 1):
+            weight_copy(way).start()
+        for way in (0, 1):
+            for role in (0, 1):
+                feature_copy(way, role).start()
+
+    def weights_to_plane():
+        for way in (0, 1):
+            weight_copy(way).wait_recv()
+
+        @pl.loop(1, CHIPS)
+        def _(k):
+            for way in (0, 1):
+                plane_copy(way, k).start()
+
+    def weights_to_mate():
+        @pl.loop(1, CHIPS)
+        def _(k):
+            for way in (0, 1):
+                plane_copy(way, k).wait_recv()
+
+        for way in (0, 1):
+            mate_copy(way).start()
+
+    def add_neighbour_features():
+        for way in (0, 1):
+            mate_copy(way).wait_recv()
+            for role in (0, 1):
+                feature_copy(way, role).wait_recv()
+
+        @pl.loop(0, NEAR // 256)
+        def _(j):
+            cols = pl.ds(pl.multiple_of(j * 256, 256), 256)
+            for way in (0, 1):
+                more = dot(cn[way], wn[way, cols, :], 1, 1)
+                for role in (0, 1):
+                    part = way if role == 0 else 1 - way
+                    dest = along(way, 3 - role)
+                    rows = pl.ds(pl.multiple_of(dest * SHARE + part * PART, PART), PART)
+                    pg[rows, cols] += more[role * PART:(role + 1) * PART]
+
+    def drain_neighbours():
+        for way in (0, 1):
+            weight_copy(way).wait_send()
+            mate_copy(way).wait_send()
+            for role in (0, 1):
+                feature_copy(way, role).wait_send()
+
+        @pl.loop(1, CHIPS)
+        def _(k):
+            for way in (0, 1):
+                plane_copy(way, k).wait_send()
+
     first(x_hop)
     for copy in loads[6:]:
         copy.start()
     for i in range(6):
         loads[i].wait()
+    to_neighbours()
 
     def partial_input_grad(start, stop):
         @pl.loop(start, stop)
@@ -274,6 +373,7 @@
     forward(x_hop, 2, 0, 1)
     partial_input_grad(3, 6)
     forward(x_hop, 2, 2, 3)
+    weights_to_plane()
     partial_input_grad(6, 9)
     forward(x_hop, 3, 0)
 
@@ -337,6 +437,7 @@
 
     forward(y_hop, 2, 0, 1, 2)
     forward(y_hop, 2, 3)
+    weights_to_mate()
     sums_into(0, 3)
     to_reducers(0)
     forward(y_hop, 3, 0)
@@ -346,6 +447,7 @@
     forward(y_hop, 3, 2, 3)
     forward(y_hop, 4, 0, 1)
     from_reducers(0)
+    add_neighbour_features()
     loads[14].wait()
     finish_ring(y_hop)
     z_first(1, 0)
@@ -418,23 +520,23 @@
         sh[rows, INTO:ALL] = high
         sl[rows, INTO:ALL] = low
 
+    z_step(2, 0)
     to_reducers(1)
+    z_step(3, 1)
     from_mate(0)
     gram_schmidt(0, into)
     from_reducers(1)
     gram_schmidt(1, into)
     gram_schmidt(2, into)
-    z_step(2, 0)
     gram_schmidt(3, into)
     to_mate(1)
     right_factors(into)
     from_mate(1)
-    z_step(3, 1)
     gram_schmidt(0, outof)
     gram_schmidt(1, outof)
+    z_step(3, 0)
     gram_schmidt(2, outof)
     gram_schmidt(3, outof)
-    z_step(3, 0)
     right_factors(outof)
 
     place = dp % 8
@@ -476,18 +578,21 @@
     def _(k):
         e_copy(k).start()
 
-    for h in (0, 1):
-        @pl.loop(0, 3)
+    def left_by_rows(start, stop):
+        @pl.loop(start, stop)
         def _(j):
-            lanes = pl.ds(pl.multiple_of(j * 384, 384), 384)
-            rows = pl.ds(pl.multiple_of(h * HALF + j * 384, 384), 384)
-            by_row = jnp.transpose(ff[h, :, lanes])
+            lanes = pl.ds(pl.multiple_of((j % 3) * 384, 384), 384)
+            rows = pl.ds(pl.multiple_of(j * 384, 384), 384)
+            by_row = jnp.transpose(ff[j // 3, :, lanes])
             pt[rows, :] = by_row
             high, low = split(by_row)
             pc[rows, 0:128] = high
             pc[rows, 128:256] = high
             pc[rows, 256:384] = low
 
+    z_step(4, 1)
+    left_by_rows(0, 2)
+
     @pl.loop(1, 8)
     def _(k):
         e_copy(k).wait_recv()
@@ -498,7 +603,7 @@
     def _(k):
         f_copy(k).start()
 
-    z_step(4, 1)
+    left_by_rows(2, 4)
 
     @pl.loop(1, 4)
     def _(k):
@@ -510,6 +615,8 @@
     def _(k):
         h_copy(k).start()
 
+    z_step(4, 0)
+    left_by_rows(4, 6)
     mine = jnp.transpose(pt[pl.ds(pl.multiple_of(dp * ROWS_P, 8), ROWS_P), :])
     for b, ref in enumerate((wide_p.at[0], narrow_p.at[0], narrow_p.at[1], wide_p.at[1])):
         ref[0] = mine[b * RANK:(b + 1) * RANK]
@@ -525,8 +632,6 @@
         qbd[b * RANK:(b + 1) * RANK, at:at + width] = high
         qbd[128 + b * RANK:128 + (b + 1) * RANK, at:at + width] = low
         qbd[256 + b * RANK:256 + (b + 1) * RANK, at:at + width] = high
-
-    z_step(4, 0)
 
     @pl.loop(0, 9)
     def _(j):
@@ -544,6 +649,7 @@
     own = pl.ds(pl.multiple_of(mp * SHARE, SHARE), SHARE)
     input_grad[...] = (pg[own, :] + rr[0, 3] + rr[1, 3]).astype(BF16)
 
+    drain_neighbours()
     drain_ring(x_hop)
     drain_ring(y_hop)
     for way in (0, 1):
@@ -604,6 +710,8 @@
             vmem((2, 4, SHARE, D), F32),
             vmem((D, ALL), BF16),
             vmem((D, ALL), BF16),
+            vmem((2, NEAR, INTO), BF16),
+            vmem((2, SHARE, INTO), BF16),
             vmem((2, 128, HALF), F32),
             vmem((128, HALF), F32),
             vmem((CHIPS - 1, 8, HALF), F32),
@@ -622,6 +730,9 @@
             sems((2, 4, 4)), sems((2, 4, 4)),
             sems((2, 4, 4)), sems((2, 4, 4)),
             sems((2, 4, 2)), sems((2, 4, 2)),
+            sems((2, 3)), sems((2, 3)),
+            sems((2, CHIPS - 1)), sems((2, CHIPS - 1)),
+            sems((2,)), sems((2,)),
             sems((2,)), sems((2,)),
             sems((2, CHIPS - 1)), sems((2, CHIPS - 1)),
             sems((2, CHIPS - 1)), sems((2, CHIPS - 1)),

time: 107 us -> 106 us (level)
    pallas_call x1, Pallas kernels: 104 us -> 103 us  [on_device(): pl.pallas_call(kernel, out_shape=tuple((pltpu.VMEM(shape, dtype) for shap...]
where the time goes in v4:
time: 106 us
  Pallas kernels  105 us (99%)
    pallas_call x1, Pallas kernels, on_device(): pl.pallas_call(kernel, out_shape=tuple((pltpu.VMEM(shape, dtype) for shap...  103 us

profile of v4, /device:TPU:1, one launch (start us, length us, event | category | flops | bytes accessed | tf_op | source)
XLA Modules:
  0.0 105.7 jit_solution(15034489857645625882)
XLA Ops:
  0.6 103.0 %shard_map.162 = (bf16[64,2304]{1,0:T(8,128)(2,1)S(1)}, f32[2,1,32,72]{3,2,1,0:T(8,128)S(1)}, f32[2,1,32,72]{3,2,1,0:T(8,128)S(1)}, f32[2,32,256]{2,1,0:T(8,128)...) custom-call(bf16[64,2304]{1,0:T(8,128)(2,1)} %x_in.1, ...), custom_call_target="tpu_custom_call" | custom-call | tf_op jit(solution)/shard_map/pallas_call | solution.py:693
  103.7 2.0 %shard_map.163 = (bf16[64,2304]{1,0:T(8,128)(2,1)}, f32[2,1,32,72]{3,2,1,0:T(8,128)}, f32[2,1,32,72]{3,2,1,0:T(8,128)}, f32[2,32,256]{2,1,0:T(8,128)}, f32[2,32,...) custom-call(bf16[64,2304]{1,0:T(8,128)(2,1)S(1)} %get-tuple-element.21.refs_0_, ...), custom_call_target="tpu_custom_call" | custom-call | tf_op jit(solution)/shard_map/pallas_call | solution.py:748

commit v5 on v4

--- a/solution.py
+++ b/solution.py
@@ -467,19 +467,26 @@
         @pl.loop(0, 8)
         def _(i):
             norms = {}
+            kept = {}
             for b in which:
                 row = [ff[h, pl.ds(b * RANK + block * 8 + i, 1), :] for h in (0, 1)]
                 for h in (0, 1):
-                    rowbuf[h, b * 8:b * 8 + 8, :] = jnp.broadcast_to(row[h], (8, HALF))
+                    wide = jnp.broadcast_to(row[h], (8, HALF))
+                    if len(which) == 1:
+                        kept[h] = wide
+                    else:
+                        rowbuf[h, b * 8:b * 8 + 8, :] = wide
                 norms[b] = jnp.sum(row[0] * row[0] + row[1] * row[1], axis=1, keepdims=True)
+            def row_of(h, b):
+                return kept[h] if kept else rowbuf[h, b * 8:b * 8 + 8, :]
+
             later = lax.broadcasted_iota(jnp.int32, (8, 1), 0) > i
             scales = {}
             for b in which:
                 for t in range(block, 4):
                     at = slice(b * RANK + t * 8, b * RANK + t * 8 + 8)
-                    r = slice(b * 8, b * 8 + 8)
                     dots = jnp.sum(
-                        ff[0, at, :] * rowbuf[0, r, :] + ff[1, at, :] * rowbuf[1, r, :],
+                        ff[0, at, :] * row_of(0, b) + ff[1, at, :] * row_of(1, b),
                         axis=1, keepdims=True,
                     )
                     scale = dots / norms[b]
@@ -488,7 +495,7 @@
                 for t in range(block, 4):
                     at = slice(b * RANK + t * 8, b * RANK + t * 8 + 8)
                     for h in (0, 1):
-                        ff[h, at, :] -= scales[b, t] * rowbuf[h, b * 8:b * 8 + 8, :]
+                        ff[h, at, :] -= scales[b, t] * row_of(h, b)
 
     def right_factors(which):
         for b in which:

time: 106 us -> 106 us (level)
  no operation moved by 1% of the time
where the time goes in v5:
time: 106 us
  Pallas kernels  105 us (99%)
    pallas_call x1, Pallas kernels, on_device(): pl.pallas_call(kernel, out_shape=tuple((pltpu.VMEM(shape, dtype) for shap...  103 us

profile of v5, /device:TPU:1, one launch (start us, length us, event | category | flops | bytes accessed | tf_op | source)
XLA Modules:
  0.0 105.7 jit_solution(3249995279674658259)
XLA Ops:
  0.6 103.0 %shard_map.162 = (bf16[64,2304]{1,0:T(8,128)(2,1)S(1)}, f32[2,1,32,72]{3,2,1,0:T(8,128)S(1)}, f32[2,1,32,72]{3,2,1,0:T(8,128)S(1)}, f32[2,32,256]{2,1,0:T(8,128)...) custom-call(bf16[64,2304]{1,0:T(8,128)(2,1)} %x_in.1, ...), custom_call_target="tpu_custom_call" | custom-call | tf_op jit(solution)/shard_map/pallas_call | solution.py:700
  103.7 2.0 %shard_map.163 = (bf16[64,2304]{1,0:T(8,128)(2,1)}, f32[2,1,32,72]{3,2,1,0:T(8,128)}, f32[2,1,32,72]{3,2,1,0:T(8,128)}, f32[2,32,256]{2,1,0:T(8,128)}, f32[2,32,...) custom-call(bf16[64,2304]{1,0:T(8,128)(2,1)S(1)} %get-tuple-element.21.refs_0_, ...), custom_call_target="tpu_custom_call" | custom-call | tf_op jit(solution)/shard_map/pallas_call | solution.py:755
